TPU v7x, 32 devices: a whole 2x2x4 slice. The times are simulated.
32 devices in a mesh: grp: 4 (over y, core), mem: 8 (over z, x).
Axes of the slice: x: 2, y: 2, z: 4, core: 2. Of those that a mesh axis runs over, the one named last changes fastest.
Arguments:
- v_stack: bfloat16 [32768, 512], P(('grp', 'mem')), may hold values from -0.1875 to 0.1875
- u_stack: bfloat16 [32768, 512], P(('grp', 'mem')), may hold values from -0.25 to 0.25
- warm_start: bfloat16 [32768, 256], P(('grp', 'mem')), may hold values from -3 to 3
- observed: bfloat16 [32768, 256], P(('grp', 'mem')), may hold values from -12 to 12, as said below
- owners: int32 [32, 4], replicated, may hold values from 0 to 31, as said below
- tile_ranks: int32 [32, 4], P(('grp', 'mem')), may hold values from 8 to 128
Outputs:
- model: float32 [32768, 256], P(('grp', 'mem'))
- residual: bfloat16 [32768, 256], P(('grp', 'mem'))
Inputs may be any that keep to these rules, and one draw needn't show every extreme that they name: Writing d = g * 8 + m, owners[d, t] = ((g + a_t) mod 4) * 8 + (m + b_t) mod 8, where the offsets a_t differ over t, the offsets b_t differ over t, some slot has a_t = 3, some slot has a_t = 2, some slot has b_t = 7 and some slot has b_t = 4. `observed`: entries of one row block share a scale.
All inputs are finite; a program needn't handle non-finite values.
Results may differ from a plain program's by a relative error of at most 0.006.
Values may be sent and summed in bfloat16 or wider, within the bound.
A program may use at most 64 MiB of HBM per device.

v0:
```python
import jax
import jax.numpy as jnp
from jax import lax
from jax.sharding import PartitionSpec as P

ITERS = 2


def pack_panels(panels, targets, peers):
    placing = (targets[:, None] == jnp.arange(peers, dtype=jnp.int32)[None, :]).astype(jnp.bfloat16)
    return jnp.einsum("tk,trh->krh", placing, panels, preferred_element_type=jnp.float32).astype(
        jnp.bfloat16
    )


def unpack_panels(received, chosen):
    return jnp.einsum(
        "kt,krh->trh", chosen.astype(jnp.bfloat16), received, preferred_element_type=jnp.float32
    ).astype(jnp.bfloat16)


def cross_groups(panels, group_steps):
    peers = lax.axis_size("grp")
    own_group = lax.axis_index("grp")
    outgoing = pack_panels(panels, (own_group + group_steps) % peers, peers)
    received = lax.all_to_all(outgoing, "grp", split_axis=0, concat_axis=0, tiled=True)
    anchors = (
        jnp.arange(peers, dtype=jnp.int32)[:, None] + group_steps[None, :]
    ) % peers == own_group
    return unpack_panels(received, anchors)


def cross_members(panels, member_steps):
    peers = lax.axis_size("mem")
    own_member = lax.axis_index("mem")
    outgoing = pack_panels(panels, (own_member + member_steps) % peers, peers)
    received = lax.all_to_all(outgoing, "mem", split_axis=0, concat_axis=0, tiled=True)
    anchors = (
        jnp.arange(peers, dtype=jnp.int32)[:, None] + member_steps[None, :]
    ) % peers == own_member
    return unpack_panels(received, anchors)


def route_panels(panels, group_steps, member_steps):
    moved = cross_groups(panels, group_steps)
    return cross_members(moved, member_steps)


def on_device(v_stack, u_stack, warm_start, observed, owners, tile_ranks):
    group_count = lax.axis_size("grp")
    member_count = lax.axis_size("mem")
    slots_held = owners.shape[1]
    stack_width = v_stack.shape[1]
    rank_cap = stack_width // slots_held
    right_count = warm_start.shape[1]
    live_rows = (
        lax.broadcasted_iota(jnp.int32, (slots_held, rank_cap), 1) < tile_ranks[0][:, None]
    ).astype(jnp.float32)
    forward_groups = owners[0] // member_count % group_count
    forward_members = owners[0] % member_count
    backward_groups = (group_count - forward_groups) % group_count
    backward_members = (member_count - forward_members) % member_count

    def forward(field):
        panels = jnp.einsum("bk,bh->kh", v_stack, field, preferred_element_type=jnp.float32)
        panels = (panels.reshape(slots_held, rank_cap, right_count) * live_rows[:, :, None]).astype(
            jnp.bfloat16
        )
        arrived = route_panels(panels, forward_groups, forward_members)
        return jnp.dot(
            u_stack, arrived.reshape(stack_width, right_count), preferred_element_type=jnp.float32
        )

    def adjoint(field):
        panels = jnp.einsum("bk,bh->kh", u_stack, field, preferred_element_type=jnp.float32)
        panels = panels.reshape(slots_held, rank_cap, right_count).astype(jnp.bfloat16)
        returned = route_panels(panels, backward_groups, backward_members)
        masked = (returned * live_rows[:, :, None]).astype(jnp.bfloat16)
        return jnp.dot(
            v_stack, masked.reshape(stack_width, right_count), preferred_element_type=jnp.float32
        )

    model = warm_start.astype(jnp.float32)
    residual = forward(warm_start) - observed.astype(jnp.float32)
    entries = float(warm_start.shape[0] * right_count * group_count * member_count)

    def iterate(index, carry):
        model, residual = carry
        spread = lax.psum(jnp.sum(jnp.abs(residual)), ("grp", "mem"))
        huber_scale = 1.345 * spread / entries + 1e-06
        weights = huber_scale / jnp.maximum(jnp.abs(residual), huber_scale)
        weighted = (weights * residual).astype(jnp.bfloat16)
        gradient = adjoint(weighted)
        grad_sum = lax.psum(jnp.sum(gradient * gradient), ("grp", "mem"))
        image_dir = forward(gradient.astype(jnp.bfloat16))
        curve_sum = lax.psum(jnp.sum(weights * image_dir * image_dir), ("grp", "mem"))
        step_size = grad_sum / (curve_sum + 1e-06)
        return (model - step_size * gradient, residual - step_size * image_dir)

    model, residual = lax.fori_loop(0, ITERS, iterate, (model, residual))
    return (model, residual.astype(jnp.bfloat16))


def solution(mesh):
    return jax.shard_map(
        on_device,
        mesh=mesh,
        in_specs=(
            P(("grp", "mem"), None),
            P(("grp", "mem"), None),
            P(("grp", "mem"), None),
            P(("grp", "mem"), None),
            P(),
            P(("grp", "mem"), None),
        ),
        out_specs=(P(("grp", "mem"), None), P(("grp", "mem"), None)),
        check_vma=False,
    )
```

profile of v0, /device:TPU:0, one launch (start us, length us, event | category | flops | bytes accessed | tf_op | source)
XLA Modules:
  0.0 359.5 jit_solution(17346770566358525864)
XLA Ops:
  2.2 1.8 fusion.178
  5.2 4.2 %all-to-all-start.4 = ((bf16[4,128,256]{2,1,0:T(8,128)(2,1)}), bf16[4,128,256]{2,1,0:T(8,128)(2,1)S(1)}, u32[]{:S(2)}, u32[]{:S(2)}) async-start(bf16[4,128,256]{2,1,0:T(8,128)(2,1)} %copy.53), calls=%async_computation.4 | async-start | bytes 524288 | tf_op jit(solution)/shard_map/all_to_all | solution.py:26
  9.5 6.0 %all-to-all-done.4 = bf16[4,128,256]{2,1,0:T(8,128)(2,1)S(1)} async-done(((bf16[4,128,256]{2,1,0:T(8,128)(2,1)}), bf16[4,128,256]{2,1,0:T(8,128)(2,1)S(1)}, u32[]{:S(2)}, u32[]{:S(2)}) %all-to-all-start.4) | async-done | bytes 262176 | tf_op jit(solution)/shard_map/all_to_all | solution.py:26
  16.9 6.5 %all-to-all-start.5 = ((bf16[8,128,256]{2,1,0:T(8,128)(2,1)}), bf16[8,128,256]{2,1,0:T(8,128)(2,1)S(1)}, u32[]{:S(2)}, u32[]{:S(2)}) async-start(bf16[8,128,256]{2,1,0:T(8,128)(2,1)} %copy.55), calls=%async_computation.5 | async-start | bytes 1048576 | tf_op jit(solution)/shard_map/all_to_all | solution.py:37
  24.7 1.1 convert_element_type.148
  25.8 12.0 %all-to-all-done.5 = bf16[8,128,256]{2,1,0:T(8,128)(2,1)S(1)} async-done(((bf16[8,128,256]{2,1,0:T(8,128)(2,1)}), bf16[8,128,256]{2,1,0:T(8,128)(2,1)S(1)}, u32[]{:S(2)}, u32[]{:S(2)}) %all-to-all-start.5) | async-done | bytes 524320 | tf_op jit(solution)/shard_map/all_to_all | solution.py:37
  40.2 316.6 %while.16 = (s32[]{:T(128)}, f32[1024,256]{0,1:T(8,128)}, f32[1024,256]{0,1:T(8,128)S(1)}, s32[4]{0:T(128)S(1)}, s32[4]{0:T(128)S(1)}, /*index=5*/bf16[1024,512]...) while((s32[]{:T(128)}, f32[1024,256]{0,1:T(8,128)}, ...), condition=%wide.region_7.8_spmd.clone, body=%wide.region_0.7_spmd.clone.sunk | while | flops 1093667328 | bytes 41949960 | solution.py:100
  41.1 38.6 %psum.37 = f32[]{:T(128)} all-reduce(f32[]{:T(128)} %abs_reduce_fusion.2), channel_id=1, replica_groups=mesh['grp'=4,'mem'=8] {'grp','mem'}, use_global_device_ids=true, to_apply=%region_2.2 | all-reduce | flops 1 | bytes 8 | tf_op jit(solution)/shard_map/while/body/eval_jaxpr/psum | solution.py:89
  82.2 3.7 %all-to-all-start = ((bf16[4,128,256]{2,1,0:T(8,128)(2,1)}), bf16[4,128,256]{2,1,0:T(8,128)(2,1)S(1)}, u32[]{:S(2)}, u32[]{:S(2)}) async-start(bf16[4,128,256]{2,1,0:T(8,128)(2,1)} %copy.103), calls=%async_computation | async-start | bytes 524288 | tf_op jit(solution)/shard_map/while/body/eval_jaxpr/all_to_all | solution.py:26
  85.9 6.0 %all-to-all-done = bf16[4,128,256]{2,1,0:T(8,128)(2,1)S(1)} async-done(((bf16[4,128,256]{2,1,0:T(8,128)(2,1)}), bf16[4,128,256]{2,1,0:T(8,128)(2,1)S(1)}, u32[]{:S(2)}, u32[]{:S(2)}) %all-to-all-start) | async-done | bytes 262176 | tf_op jit(solution)/shard_map/while/body/eval_jaxpr/all_to_all | solution.py:26
  92.5 0.9 copy.104
  93.4 4.2 %all-to-all-start.1 = ((bf16[8,128,256]{2,1,0:T(8,128)(2,1)}), bf16[8,128,256]{2,1,0:T(8,128)(2,1)S(1)}, u32[]{:S(2)}, u32[]{:S(2)}) async-start(bf16[8,128,256]{2,1,0:T(8,128)(2,1)} %copy.104), calls=%async_computation.1 | async-start | bytes 1048576 | tf_op jit(solution)/shard_map/while/body/eval_jaxpr/all_to_all | solution.py:37
  97.6 14.3 %all-to-all-done.1 = bf16[8,128,256]{2,1,0:T(8,128)(2,1)S(1)} async-done(((bf16[8,128,256]{2,1,0:T(8,128)(2,1)}), bf16[8,128,256]{2,1,0:T(8,128)(2,1)S(1)}, u32[]{:S(2)}, u32[]{:S(2)}) %all-to-all-start.1) | async-done | bytes 524320 | tf_op jit(solution)/shard_map/while/body/eval_jaxpr/all_to_all | solution.py:37
  112.4 1.2 multiply_reduce_fusion.2
  113.6 1.2 convolution_bitcast_fusion.4
  114.8 2.0 copy.106
  116.9 1.5 convolution_convert_fusion.20
  119.1 3.4 all-to-all-start.2
  122.5 6.0 %all-to-all-done.2 = bf16[4,128,256]{2,1,0:T(8,128)(2,1)S(1)} async-done(((bf16[4,128,256]{2,1,0:T(8,128)(2,1)}), bf16[4,128,256]{2,1,0:T(8,128)(2,1)S(1)}, u32[]{:S(2)}, u32[]{:S(2)}) %all-to-all-start.2) | async-done | bytes 262176 | tf_op jit(solution)/shard_map/while/body/eval_jaxpr/all_to_all | solution.py:26
  128.5 1.3 convolution_convert_fusion.21
  129.8 1.9 copy.108
  131.8 4.1 %all-to-all-start.3 = ((bf16[8,128,256]{2,1,0:T(8,128)(2,1)}), bf16[8,128,256]{2,1,0:T(8,128)(2,1)}, u32[]{:S(2)}, u32[]{:S(2)}) async-start(bf16[8,128,256]{2,1,0:T(8,128)(2,1)} %copy.108), calls=%async_computation.3 | async-start | bytes 1048576 | tf_op jit(solution)/shard_map/while/body/eval_jaxpr/all_to_all | solution.py:37
  135.9 14.6 %all-to-all-done.3 = bf16[8,128,256]{2,1,0:T(8,128)(2,1)} async-done(((bf16[8,128,256]{2,1,0:T(8,128)(2,1)}), bf16[8,128,256]{2,1,0:T(8,128)(2,1)}, u32[]{:S(2)}, u32[]{:S(2)}) %all-to-all-start.3) | async-done | bytes 524320 | tf_op jit(solution)/shard_map/while/body/eval_jaxpr/all_to_all | solution.py:37
  150.5 1.6 convolution_convert_fusion.22
  152.1 2.1 fusion.239
  154.2 38.7 %all-reduce.2 = (f32[]{:T(128)}, f32[]{:T(128)}) all-reduce(f32[]{:T(128)} %get-tuple-element.303, f32[]{:T(128)} %get-tuple-element.304), channel_id=1, replica_groups=mesh['grp'=4,'mem'=8] {'grp','mem'}, use_global_device_ids=true, to_apply=%region_4.4 | all-reduce | flops 2 | bytes 16 | tf_op jit(solution)/shard_map/while/body/eval_jaxpr/psum | solution.py:94
  194.2 3.1 bitcast_subtract_fusion.2
  198.1 41.1 %psum.37 = f32[]{:T(128)} all-reduce(f32[]{:T(128)} %abs_reduce_fusion.2), channel_id=1, replica_groups=mesh['grp'=4,'mem'=8] {'grp','mem'}, use_global_device_ids=true, to_apply=%region_2.2 | all-reduce | flops 1 | bytes 8 | tf_op jit(solution)/shard_map/while/body/eval_jaxpr/psum | solution.py:89
  241.7 3.7 %all-to-all-start = ((bf16[4,128,256]{2,1,0:T(8,128)(2,1)}), bf16[4,128,256]{2,1,0:T(8,128)(2,1)S(1)}, u32[]{:S(2)}, u32[]{:S(2)}) async-start(bf16[4,128,256]{2,1,0:T(8,128)(2,1)} %copy.103), calls=%async_computation | async-start | bytes 524288 | tf_op jit(solution)/shard_map/while/body/eval_jaxpr/all_to_all | solution.py:26
  245.5 6.0 %all-to-all-done = bf16[4,128,256]{2,1,0:T(8,128)(2,1)S(1)} async-done(((bf16[4,128,256]{2,1,0:T(8,128)(2,1)}), bf16[4,128,256]{2,1,0:T(8,128)(2,1)S(1)}, u32[]{:S(2)}, u32[]{:S(2)}) %all-to-all-start) | async-done | bytes 262176 | tf_op jit(solution)/shard_map/while/body/eval_jaxpr/all_to_all | solution.py:26
  252.9 4.2 %all-to-all-start.1 = ((bf16[8,128,256]{2,1,0:T(8,128)(2,1)}), bf16[8,128,256]{2,1,0:T(8,128)(2,1)S(1)}, u32[]{:S(2)}, u32[]{:S(2)}) async-start(bf16[8,128,256]{2,1,0:T(8,128)(2,1)} %copy.104), calls=%async_computation.1 | async-start | bytes 1048576 | tf_op jit(solution)/shard_map/while/body/eval_jaxpr/all_to_all | solution.py:37
  257.1 14.3 %all-to-all-done.1 = bf16[8,128,256]{2,1,0:T(8,128)(2,1)S(1)} async-done(((bf16[8,128,256]{2,1,0:T(8,128)(2,1)}), bf16[8,128,256]{2,1,0:T(8,128)(2,1)S(1)}, u32[]{:S(2)}, u32[]{:S(2)}) %all-to-all-start.1) | async-done | bytes 524320 | tf_op jit(solution)/shard_map/while/body/eval_jaxpr/all_to_all | solution.py:37
  271.9 1.2 multiply_reduce_fusion.2
  273.1 1.2 convolution_bitcast_fusion.4
  274.4 2.0 copy.106
  276.4 1.5 convolution_convert_fusion.20
  278.7 3.4 all-to-all-start.2
  282.1 6.0 %all-to-all-done.2 = bf16[4,128,256]{2,1,0:T(8,128)(2,1)S(1)} async-done(((bf16[4,128,256]{2,1,0:T(8,128)(2,1)}), bf16[4,128,256]{2,1,0:T(8,128)(2,1)S(1)}, u32[]{:S(2)}, u32[]{:S(2)}) %all-to-all-start.2) | async-done | bytes 262176 | tf_op jit(solution)/shard_map/while/body/eval_jaxpr/all_to_all | solution.py:26
  288.1 1.3 convolution_convert_fusion.21
  289.4 1.9 copy.108
  291.3 4.1 %all-to-all-start.3 = ((bf16[8,128,256]{2,1,0:T(8,128)(2,1)}), bf16[8,128,256]{2,1,0:T(8,128)(2,1)}, u32[]{:S(2)}, u32[]{:S(2)}) async-start(bf16[8,128,256]{2,1,0:T(8,128)(2,1)} %copy.108), calls=%async_computation.3 | async-start | bytes 1048576 | tf_op jit(solution)/shard_map/while/body/eval_jaxpr/all_to_all | solution.py:37
  295.5 14.6 %all-to-all-done.3 = bf16[8,128,256]{2,1,0:T(8,128)(2,1)} async-done(((bf16[8,128,256]{2,1,0:T(8,128)(2,1)}), bf16[8,128,256]{2,1,0:T(8,128)(2,1)}, u32[]{:S(2)}, u32[]{:S(2)}) %all-to-all-start.3) | async-done | bytes 524320 | tf_op jit(solution)/shard_map/while/body/eval_jaxpr/all_to_all | solution.py:37
  310.1 1.6 convolution_convert_fusion.22
  311.7 2.1 fusion.239
  313.7 38.7 %all-reduce.2 = (f32[]{:T(128)}, f32[]{:T(128)}) all-reduce(f32[]{:T(128)} %get-tuple-element.303, f32[]{:T(128)} %get-tuple-element.304), channel_id=1, replica_groups=mesh['grp'=4,'mem'=8] {'grp','mem'}, use_global_device_ids=true, to_apply=%region_4.4 | all-reduce | flops 2 | bytes 16 | tf_op jit(solution)/shard_map/while/body/eval_jaxpr/psum | solution.py:94
  353.7 3.1 bitcast_subtract_fusion.2
  356.8 1.0 copy.59
  358.2 1.3 copy.60
  (69 shorter events, 18.0 us)
Async XLA Ops:
  0.6 0.7 copy-start.8
  1.5 0.7 copy-start.7
  5.2 10.3 %all-to-all-start.4 = ((bf16[4,128,256]{2,1,0:T(8,128)(2,1)}), bf16[4,128,256]{2,1,0:T(8,128)(2,1)S(1)}, u32[]{:S(2)}, u32[]{:S(2)}) async-start(bf16[4,128,256]{2,1,0:T(8,128)(2,1)} %copy.53), calls=%async_computation.4 | async-start | bytes 524288 | tf_op jit(solution)/shard_map/all_to_all | solution.py:26
  16.9 6.5 %copy-start.5 = (bf16[1024,256]{1,0:T(8,128)(2,1)S(1)}, bf16[1024,256]{1,0:T(8,128)(2,1)}, u32[]{:S(2)}) copy-start(bf16[1024,256]{1,0:T(8,128)(2,1)} %param.10) | copy-start | bytes 1572868
  16.9 20.8 %all-to-all-start.5 = ((bf16[8,128,256]{2,1,0:T(8,128)(2,1)}), bf16[8,128,256]{2,1,0:T(8,128)(2,1)S(1)}, u32[]{:S(2)}, u32[]{:S(2)}) async-start(bf16[8,128,256]{2,1,0:T(8,128)(2,1)} %copy.55), calls=%async_computation.5 | async-start | bytes 1048576 | tf_op jit(solution)/shard_map/all_to_all | solution.py:37
  23.5 1.0 copy-start.6
  37.8 1.2 copy-start.2
  39.0 1.2 copy-start
  40.2 40.2 %copy-start.3 = (bf16[1024,512]{1,0:T(8,128)(2,1)S(1)}, bf16[1024,512]{1,0:T(8,128)(2,1)}, u32[]{:S(2)}) copy-start(bf16[1024,512]{1,0:T(8,128)(2,1)} %get-tuple-element.345) | copy-start | bytes 3145732 | tf_op jit(solution)/shard_map/while
  82.2 9.8 %all-to-all-start = ((bf16[4,128,256]{2,1,0:T(8,128)(2,1)}), bf16[4,128,256]{2,1,0:T(8,128)(2,1)S(1)}, u32[]{:S(2)}, u32[]{:S(2)}) async-start(bf16[4,128,256]{2,1,0:T(8,128)(2,1)} %copy.103), calls=%async_computation | async-start | bytes 524288 | tf_op jit(solution)/shard_map/while/body/eval_jaxpr/all_to_all | solution.py:26
  93.4 18.5 %all-to-all-start.1 = ((bf16[8,128,256]{2,1,0:T(8,128)(2,1)}), bf16[8,128,256]{2,1,0:T(8,128)(2,1)S(1)}, u32[]{:S(2)}, u32[]{:S(2)}) async-start(bf16[8,128,256]{2,1,0:T(8,128)(2,1)} %copy.104), calls=%async_computation.1 | async-start | bytes 1048576 | tf_op jit(solution)/shard_map/while/body/eval_jaxpr/all_to_all | solution.py:37
  119.1 9.4 %all-to-all-start.2 = ((bf16[4,128,256]{2,1,0:T(8,128)(2,1)}), bf16[4,128,256]{2,1,0:T(8,128)(2,1)S(1)}, u32[]{:S(2)}, u32[]{:S(2)}) async-start(bf16[4,128,256]{2,1,0:T(8,128)(2,1)} %copy.107), calls=%async_computation.2 | async-start | bytes 524288 | tf_op jit(solution)/shard_map/while/body/eval_jaxpr/all_to_all | solution.py:26
  131.8 18.7 %all-to-all-start.3 = ((bf16[8,128,256]{2,1,0:T(8,128)(2,1)}), bf16[8,128,256]{2,1,0:T(8,128)(2,1)}, u32[]{:S(2)}, u32[]{:S(2)}) async-start(bf16[8,128,256]{2,1,0:T(8,128)(2,1)} %copy.108), calls=%async_computation.3 | async-start | bytes 1048576 | tf_op jit(solution)/shard_map/while/body/eval_jaxpr/all_to_all | solution.py:37
  150.5 1.6 copy-start.4
  197.3 42.7 %copy-start.3 = (bf16[1024,512]{1,0:T(8,128)(2,1)S(1)}, bf16[1024,512]{1,0:T(8,128)(2,1)}, u32[]{:S(2)}) copy-start(bf16[1024,512]{1,0:T(8,128)(2,1)} %get-tuple-element.345) | copy-start | bytes 3145732 | tf_op jit(solution)/shard_map/while
  241.7 9.8 %all-to-all-start = ((bf16[4,128,256]{2,1,0:T(8,128)(2,1)}), bf16[4,128,256]{2,1,0:T(8,128)(2,1)S(1)}, u32[]{:S(2)}, u32[]{:S(2)}) async-start(bf16[4,128,256]{2,1,0:T(8,128)(2,1)} %copy.103), calls=%async_computation | async-start | bytes 524288 | tf_op jit(solution)/shard_map/while/body/eval_jaxpr/all_to_all | solution.py:26
  252.9 18.5 %all-to-all-start.1 = ((bf16[8,128,256]{2,1,0:T(8,128)(2,1)}), bf16[8,128,256]{2,1,0:T(8,128)(2,1)S(1)}, u32[]{:S(2)}, u32[]{:S(2)}) async-start(bf16[8,128,256]{2,1,0:T(8,128)(2,1)} %copy.104), calls=%async_computation.1 | async-start | bytes 1048576 | tf_op jit(solution)/shard_map/while/body/eval_jaxpr/all_to_all | solution.py:37
  278.7 9.4 %all-to-all-start.2 = ((bf16[4,128,256]{2,1,0:T(8,128)(2,1)}), bf16[4,128,256]{2,1,0:T(8,128)(2,1)S(1)}, u32[]{:S(2)}, u32[]{:S(2)}) async-start(bf16[4,128,256]{2,1,0:T(8,128)(2,1)} %copy.107), calls=%async_computation.2 | async-start | bytes 524288 | tf_op jit(solution)/shard_map/while/body/eval_jaxpr/all_to_all | solution.py:26
  291.3 18.7 %all-to-all-start.3 = ((bf16[8,128,256]{2,1,0:T(8,128)(2,1)}), bf16[8,128,256]{2,1,0:T(8,128)(2,1)}, u32[]{:S(2)}, u32[]{:S(2)}) async-start(bf16[8,128,256]{2,1,0:T(8,128)(2,1)} %copy.108), calls=%async_computation.3 | async-start | bytes 1048576 | tf_op jit(solution)/shard_map/while/body/eval_jaxpr/all_to_all | solution.py:37
  310.1 1.6 copy-start.4
  356.8 1.4 copy-start.1
where the time goes:
time: 361 us; the launch traced here: 360 us
  blocking collectives  157 us (43%)
  waiting for transfers between devices  99.7 us (28%)
  starting transfers between devices  41.7 us (12%)
  matrix products  25 us (7%)
  local copies, waits for them, and re-layouts  21.8 us (6%)
  other arithmetic  9.32 us (3%)
  loops' own time  4.11 us (1%)
    psum x2, blocking collectives, iterate(): spread = lax.psum(jnp.sum(jnp.abs(residual)), ('grp', 'mem'))  79.8 us
    psum x2, blocking collectives, iterate(): grad_sum = lax.psum(jnp.sum(gradient * gradient), ('grp', 'mem'))  77.4 us
    all_to_all x5, waiting for transfers between devices, cross_members(): lax.all_to_all(outgoing, 'mem', split_axis=0, concat_axis=0, tiled=True)  69.7 us
    all_to_all x5, waiting for transfers between devices, cross_groups(): lax.all_to_all(outgoing, 'grp', split_axis=0, concat_axis=0, tiled=True)  30.1 us
    all_to_all x5, starting transfers between devices, cross_members(): lax.all_to_all(outgoing, 'mem', split_axis=0, concat_axis=0, tiled=True)  23.2 us
    all_to_all x5, starting transfers between devices, cross_groups(): lax.all_to_all(outgoing, 'grp', split_axis=0, concat_axis=0, tiled=True)  18.5 us
    convert_element_type x10, local copies, waits for them, and re-layouts, pack_panels(): jnp.einsum('tk,trh->krh', placing, panels, preferred_element_type=jnp.flo...  10.2 us
    dot_general x10, matrix products, pack_panels(): jnp.einsum('tk,trh->krh', placing, panels, preferred_element_type=jnp.flo...  8.2 us
  transfers between devices with their start and end apart: 10, of which 10 were waited for; matrix products, arithmetic and copies ran while one was open for 0% of the time, Pallas kernels for 0%

commit v1 on v0

v1 whole, which is shorter than its diff:
```python
import functools

import jax
import jax.numpy as jnp
from jax import lax
from jax.experimental import pallas as pl
from jax.experimental.pallas import tpu as pltpu
from jax.sharding import PartitionSpec as P

ITERS = 2
ROUTES = 1 + 2 * ITERS
SUMS = 2 * ITERS
CHUNK = 256
MESH = pl.DeviceIdType.MESH


def kernel(dims, offsets, tab_ref, rank_ref, v_ref, u_ref, x_ref, obs_ref, model_ref, out_ref,
           vt, ut, resid, weight, grad, image, field, zbuf, arrived, part, *rest):
    groups, members, slots, width, rows, cols = dims
    devices = groups * members
    count = len(offsets)
    gsend, rest = rest[:ROUTES], rest[ROUTES:]
    gbuf, rest = rest[:ROUTES], rest[ROUTES:]
    msend, rest = rest[:ROUTES], rest[ROUTES:]
    mbuf, rest = rest[:ROUTES], rest[ROUTES:]
    sums, rest = rest[:SUMS], rest[SUMS:]
    gs_sem, gr_sem, ms_sem, mr_sem, ss_sem, sr_sem = rest
    g = lax.axis_index("grp")
    m = lax.axis_index("mem")

    def peer(r):
        return (lax.rem(g + lax.div(r, members), groups), lax.rem(m + lax.rem(r, members), members))

    barrier = pltpu.get_barrier_semaphore()

    @pl.loop(1, devices)
    def _(r):
        pl.semaphore_signal(barrier, inc=1, device_id=peer(r), device_id_type=MESH)

    ranks = [rank_ref[0, t] for t in range(slots)]

    def total(values):
        return functools.reduce(lambda p, q: p + q, values)

    group_slot = [tab_ref[0, s] for s in range(groups)]
    member_src = [tab_ref[0, groups + k] for k in range(count)]
    place = [tab_ref[0, groups + count + t] for t in range(slots)]

    row_ids = lax.broadcasted_iota(jnp.int32, (width, cols), 0)
    live = [jnp.minimum(jnp.maximum(ranks[t] - row_ids, 0), 1).astype(jnp.float32) for t in range(slots)]
    pending = []

    def at(i):
        return pl.ds(i * CHUNK, CHUNK)

    chunks = rows // CHUNK

    def send(src, dst, send_sem, recv_sem, target):
        copy = pltpu.make_async_remote_copy(
            src_ref=src, dst_ref=dst, send_sem=send_sem, recv_sem=recv_sem,
            device_id=target, device_id_type=MESH)
        copy.start()
        pending.append(copy)
        return copy

    def route(i, back, meanwhile=None):
        copies = []
        for s in reversed(range(groups)):
            panel = zbuf[group_slot[s]]
            if s == 0:
                gbuf[i][0] = panel
            else:
                gsend[i][s] = panel
                step = groups - s if back else s
                copies.append(send(gsend[i].at[s], gbuf[i].at[s], gs_sem.at[i, s], gr_sem.at[i, s],
                                   (lax.rem(g + step, groups), m)))
        if meanwhile is not None:
            meanwhile()
        for copy in copies:
            copy.wait_recv()
        copies = []
        for k, o in enumerate(offsets):
            panel = gbuf[i][member_src[k]]
            if o == 0:
                mbuf[i][k] = panel
            else:
                msend[i][k] = panel
                step = members - o if back else o
                copies.append(send(msend[i].at[k], mbuf[i].at[k], ms_sem.at[i, k], mr_sem.at[i, k],
                                   (g, lax.rem(m + step, members))))
        for copy in copies:
            copy.wait_recv()
        for t in range(slots):
            panel = mbuf[i][place[t]]
            if back:
                panel = panel * live[t].astype(jnp.bfloat16)
            arrived[t * width:(t + 1) * width, :] = panel

    def fold(x):
        y = jnp.sum(x.reshape(x.shape[0] // 8, 8, cols), axis=0)
        return total(y[:, c:c + 128] for c in range(0, cols, 128))

    def all_sum(j, values):
        n = len(values)
        for q, value in enumerate(values):
            sums[j][0, q * 8:(q + 1) * 8] = value

        def put(r):
            return pltpu.make_async_remote_copy(
                src_ref=sums[j].at[0], dst_ref=sums[j].at[r], send_sem=ss_sem.at[j],
                recv_sem=sr_sem.at[j], device_id=peer(r), device_id_type=MESH)

        @pl.loop(1, devices)
        def _(r):
            put(r).start()

        rest_of = sums[j].at[pl.ds(1, devices - 1)]
        whole = pltpu.make_async_remote_copy(
            src_ref=rest_of, dst_ref=rest_of, send_sem=ss_sem.at[j],
            recv_sem=sr_sem.at[j], device_id=peer(1), device_id_type=MESH)
        whole.wait_recv()
        pending.append(whole)
        added = jnp.sum(sums[j][...], axis=0)
        return [jnp.sum(added[q * 8:(q + 1) * 8]) for q in range(n)]

    def project(basis_t, value_ref):
        return jnp.dot(basis_t[...], value_ref[...], preferred_element_type=jnp.float32)

    def project_forward(value_ref):
        z = project(vt, value_ref)
        for t in range(slots):
            panel = z[t * width:(t + 1) * width]
            zbuf[t] = (panel * live[t]).astype(jnp.bfloat16)

    def apply(basis, i):
        return jnp.dot(basis[at(i), :], arrived[...], preferred_element_type=jnp.float32)

    def transpose_u():
        ut[...] = u_ref[...].T

    vt[...] = v_ref[...].T
    project_forward(x_ref)
    pl.semaphore_wait(barrier, devices - 1)
    route(0, False, transpose_u)
    part_sum = jnp.zeros((8, 128), jnp.float32)
    for i in range(chunks):
        r = apply(u_ref, i) - obs_ref[at(i), :].astype(jnp.float32)
        resid[at(i), :] = r
        part_sum = part_sum + fold(jnp.abs(r))

    entries = float(rows * cols * devices)
    for it in range(ITERS):
        (spread,) = all_sum(2 * it, [part_sum])
        scale = 1.345 * spread / entries + 1e-06
        for i in range(chunks):
            r = resid[at(i), :]
            w = scale / jnp.maximum(jnp.abs(r), scale)
            weight[at(i), :] = w
            field[at(i), :] = (w * r).astype(jnp.bfloat16)
        z = project(ut, field).astype(jnp.bfloat16)
        for t in range(slots):
            zbuf[t] = z[t * width:(t + 1) * width]
        route(1 + 2 * it, True)
        grad_part = jnp.zeros((8, 128), jnp.float32)
        for i in range(chunks):
            d = apply(v_ref, i)
            grad[at(i), :] = d
            field[at(i), :] = d.astype(jnp.bfloat16)
        project_forward(field)

        def square():
            acc = jnp.zeros((8, 128), jnp.float32)
            for i in range(chunks):
                d = grad[at(i), :]
                acc = acc + fold(d * d)
            part[...] = acc

        route(2 + 2 * it, False, square)
        curve_part = jnp.zeros((8, 128), jnp.float32)
        for i in range(chunks):
            y = apply(u_ref, i)
            image[at(i), :] = y
            curve_part = curve_part + fold(weight[at(i), :] * y * y)
        grad_sum, curve_sum = all_sum(2 * it + 1, [part[...], curve_part])
        step = grad_sum / (curve_sum + 1e-06)
        part_sum = jnp.zeros((8, 128), jnp.float32)
        for i in range(chunks):
            r = resid[at(i), :] - step * image[at(i), :]
            if it < ITERS - 1:
                resid[at(i), :] = r
                part_sum = part_sum + fold(jnp.abs(r))
            else:
                out_ref[at(i), :] = r.astype(jnp.bfloat16)
            before = x_ref[at(i), :].astype(jnp.float32) if it == 0 else model_ref[at(i), :]
            model_ref[at(i), :] = before - step * grad[at(i), :]
    for copy in pending:
        copy.wait_send()


def on_device(groups, members, v_stack, u_stack, warm_start, observed, owners, tile_ranks):
    rows, stack = v_stack.shape
    cols = warm_start.shape[1]
    slots = owners.shape[1]
    width = stack // slots
    devices = groups * members
    offsets = tuple(range(members))
    dims = (groups, members, slots, width, rows, cols)
    f32, bf16 = jnp.float32, jnp.bfloat16
    vmem = pl.BlockSpec(memory_space=pltpu.VMEM)
    smem = pl.BlockSpec(memory_space=pltpu.SMEM)
    dma = pltpu.SemaphoreType.DMA
    count = len(offsets)
    scratch = [
        pltpu.VMEM((stack, rows), bf16), pltpu.VMEM((stack, rows), bf16),
        pltpu.VMEM((rows, cols), f32), pltpu.VMEM((rows, cols), f32),
        pltpu.VMEM((rows, cols), f32), pltpu.VMEM((rows, cols), f32),
        pltpu.VMEM((rows, cols), bf16), pltpu.VMEM((slots, width, cols), bf16),
        pltpu.VMEM((stack, cols), bf16), pltpu.VMEM((8, 128), f32),
    ]
    scratch += [pltpu.VMEM((groups, width, cols), bf16)] * (2 * ROUTES)
    scratch += [pltpu.VMEM((count, width, cols), bf16)] * (2 * ROUTES)
    scratch += [pltpu.VMEM((devices, 8 * (1 + j % 2), 128), f32) for j in range(SUMS)]
    scratch += [dma((ROUTES, groups)), dma((ROUTES, groups)), dma((ROUTES, count)), dma((ROUTES, count)),
                dma((SUMS,)), dma((SUMS,))]
    lead = owners[0] // members
    shift = owners[0] % members
    slot_ids = jnp.arange(slots, dtype=jnp.int32)
    member_hit = (shift[:, None] == jnp.array(offsets, jnp.int32)[None, :]).astype(jnp.int32)
    group_hit = (lead[:, None] == jnp.arange(groups, dtype=jnp.int32)[None, :]).astype(jnp.int32)
    table = jnp.concatenate([
        jnp.sum(group_hit * slot_ids[:, None], axis=0),
        jnp.sum(member_hit * lead[:, None], axis=0),
        jnp.sum(member_hit * jnp.arange(count, dtype=jnp.int32)[None, :], axis=1),
    ])[None, :]
    return pl.pallas_call(
        functools.partial(kernel, dims, offsets),
        out_shape=(jax.ShapeDtypeStruct((rows, cols), f32), jax.ShapeDtypeStruct((rows, cols), bf16)),
        in_specs=[smem, smem, vmem, vmem, vmem, vmem],
        out_specs=(vmem, vmem),
        scratch_shapes=scratch,
        compiler_params=pltpu.CompilerParams(
            collective_id=0, has_side_effects=True, vmem_limit_bytes=60 * 1024 * 1024),
        cost_estimate=pl.CostEstimate(flops=10 * 2 * rows * stack * cols, bytes_accessed=8 * rows * stack, transcendentals=0),
    )(table, tile_ranks, v_stack, u_stack, warm_start, observed)


def solution(mesh):
    split = P(("grp", "mem"), None)
    return jax.shard_map(
        functools.partial(on_device, mesh.shape["grp"], mesh.shape["mem"]),
        mesh=mesh,
        in_specs=(split, split, split, split, P(), split),
        out_specs=(split, split),
        check_vma=False,
    )
```

time: 361 us -> 133 us (0.37)
  blocking collectives: 157 us -> 0 us
  Pallas kernels: 0 us -> 128 us
  waiting for transfers between devices: 99.7 us -> 0 us
  starting transfers between devices: 41.7 us -> 0 us
  matrix products: 25 us -> 0 us
  local copies, waits for them, and re-layouts: 21.8 us -> 3.91 us
  other arithmetic: 9.32 us -> 0.88 us
  loops' own time: 4.11 us -> 0 us
    psum x4 -> x0, blocking collectives: 157 us -> none  [the longest x2 79.8 us: iterate(): spread = lax.psum(jnp.sum(jnp.abs(residual)), ('grp', 'mem'))]
    pallas_call x0 -> x1, Pallas kernels: none -> 128 us  [on_device(): pl.pallas_call(functools.partial(kernel, dims, offsets), out_shape=(jax.S...]
    all_to_all x10 -> x0, waiting for transfers between devices: 99.7 us -> none  [the longest x5 69.7 us: cross_members(): lax.all_to_all(outgoing, 'mem', split_axis=0, concat_axis=0, tiled=True)]
    all_to_all x10 -> x0, starting transfers between devices: 41.7 us -> none  [the longest x5 23.2 us: cross_members(): lax.all_to_all(outgoing, 'mem', split_axis=0, concat_axis=0, tiled=True)]
    dot_general x25 -> x0, matrix products: 25 us -> none  [the longest x10 8.2 us: pack_panels(): jnp.einsum('tk,trh->krh', placing, panels, preferred_element_type=jnp.flo...]
    convert_element_type x19 -> x0, local copies, waits for them, and re-layouts: 11 us -> none  [the longest x10 10.2 us: pack_panels(): jnp.einsum('tk,trh->krh', placing, panels, preferred_element_type=jnp.flo...]
    sub x2 -> x0, other arithmetic: 6.19 us -> none  [iterate(): return (model - step_size * gradient, residual - step_size * image_dir)]
    another operation x1 -> x0, loops' own time: 4.11 us -> none  [on_device(): model, residual = lax.fori_loop(0, ITERS, iterate, (model, residual))]
  transfers between devices with their start and end apart: 10 -> 0, of which waited for: 10 -> 0; matrix products, arithmetic and copies ran while one was open for 0% -> 0% of each run, Pallas kernels for 0% -> 0%
where the time goes in v1:
time: 133 us
  Pallas kernels  128 us (96%)
  local copies, waits for them, and re-layouts  3.91 us (3%)
    pallas_call x1, Pallas kernels, on_device(): pl.pallas_call(functools.partial(kernel, dims, offsets), out_shape=(jax.S...  128 us
    unnamed x4, local copies, waits for them, and re-layouts  3.12 us

profile of v1, /device:TPU:0, one launch (start us, length us, event | category | flops | bytes accessed | tf_op | source)
XLA Modules:
  0.0 133.0 jit_solution(9661422094252661810)
XLA Ops:
  0.6 0.8 slice_reduce_fusion
  1.4 0.1 select_reduce_fusion
  1.5 0.2 fusion.2
  1.7 0.6 add_bitcast_fusion.tab_ref
  2.3 127.5 %shard_map.86 = (f32[1024,256]{1,0:T(8,128)}, bf16[1024,256]{1,0:T(8,128)(2,1)}) custom-call(s32[1,16]{1,0:T(1,128)} %add_bitcast_fusion.tab_ref, s32[1,4]{1,0:T(1,128)} %rank_ref.1, bf16[1024,512]{1,0:T(8,128)(2,1)} %v_ref.1, bf16[1024,512]{1,0:T(8,128)(2,1)} %u_ref.1, bf16[1024,256]{1,0:T(8,128)(2,1)} %x_ref.1, bf16[1024,256]{1,0:T(8,128)(2,1)} %obs_ref.1), custom_call_target="tpu_custom_call" | custom-call | flops 2684354560 | bytes 4194304 | tf_op jit(solution)/shard_map/pallas_call | solution.py:235
  129.9 0.0 copy-start
  129.9 2.3 %copy.11 = f32[1024,256]{1,0:T(8,128)} copy(f32[1024,256]{1,0:T(8,128)} %get-tuple-element.8) | data formatting | bytes 2097152
  132.2 0.0 copy-done
  132.2 0.8 copy.12
  (1 shorter events, 0.0 us)
Async XLA Ops:
  129.9 2.3 %copy-start = (bf16[1024,256]{1,0:T(8,128)(2,1)S(1)}, bf16[1024,256]{1,0:T(8,128)(2,1)}, u32[]{:S(2)}) copy-start(bf16[1024,256]{1,0:T(8,128)(2,1)} %get-tuple-element.9) | copy-start | bytes 1572868

commit v2 on v1

--- a/solution.py
+++ b/solution.py
@@ -11,6 +11,8 @@
 ROUTES = 1 + 2 * ITERS
 SUMS = 2 * ITERS
 CHUNK = 256
+HALVES = 1
+PARTS = ROUTES * HALVES
 MESH = pl.DeviceIdType.MESH
 
 
@@ -19,16 +21,18 @@
     groups, members, slots, width, rows, cols = dims
     devices = groups * members
     count = len(offsets)
-    gsend, rest = rest[:ROUTES], rest[ROUTES:]
-    gbuf, rest = rest[:ROUTES], rest[ROUTES:]
-    msend, rest = rest[:ROUTES], rest[ROUTES:]
-    mbuf, rest = rest[:ROUTES], rest[ROUTES:]
+    gsend, rest = rest[:PARTS], rest[PARTS:]
+    gbuf, rest = rest[:PARTS], rest[PARTS:]
+    msend, rest = rest[:PARTS], rest[PARTS:]
+    mbuf, rest = rest[:PARTS], rest[PARTS:]
     sums, rest = rest[:SUMS], rest[SUMS:]
     gs_sem, gr_sem, ms_sem, mr_sem, ss_sem, sr_sem = rest
     g = lax.axis_index("grp")
     m = lax.axis_index("mem")
 
     def peer(r):
+        if isinstance(r, int):
+            return (lax.rem(g + r // members, groups), lax.rem(m + r % members, members))
         return (lax.rem(g + lax.div(r, members), groups), lax.rem(m + lax.rem(r, members), members))
 
     barrier = pltpu.get_barrier_semaphore()
@@ -54,6 +58,9 @@
         return pl.ds(i * CHUNK, CHUNK)
 
     chunks = rows // CHUNK
+
+    def lanes(h):
+        return slice(h * (cols // HALVES), (h + 1) * (cols // HALVES))
 
     def send(src, dst, send_sem, recv_sem, target):
         copy = pltpu.make_async_remote_copy(
@@ -64,37 +71,47 @@
         return copy
 
     def route(i, back, meanwhile=None):
-        copies = []
-        for s in reversed(range(groups)):
-            panel = zbuf[group_slot[s]]
-            if s == 0:
-                gbuf[i][0] = panel
-            else:
-                gsend[i][s] = panel
-                step = groups - s if back else s
-                copies.append(send(gsend[i].at[s], gbuf[i].at[s], gs_sem.at[i, s], gr_sem.at[i, s],
-                                   (lax.rem(g + step, groups), m)))
+        sent = []
+        for h in range(HALVES):
+            q = i * HALVES + h
+            copies = []
+            for s in reversed(range(groups)):
+                panel = zbuf[group_slot[s], :, lanes(h)]
+                if s == 0:
+                    gbuf[q][0] = panel
+                else:
+                    gsend[q][s] = panel
+                    step = groups - s if back else s
+                    copies.append(send(gsend[q].at[s], gbuf[q].at[s], gs_sem.at[q, s], gr_sem.at[q, s],
+                                       (lax.rem(g + step, groups), m)))
+            sent.append(copies)
         if meanwhile is not None:
             meanwhile()
-        for copy in copies:
-            copy.wait_recv()
-        copies = []
-        for k, o in enumerate(offsets):
-            panel = gbuf[i][member_src[k]]
-            if o == 0:
-                mbuf[i][k] = panel
-            else:
-                msend[i][k] = panel
-                step = members - o if back else o
-                copies.append(send(msend[i].at[k], mbuf[i].at[k], ms_sem.at[i, k], mr_sem.at[i, k],
-                                   (g, lax.rem(m + step, members))))
-        for copy in copies:
-            copy.wait_recv()
-        for t in range(slots):
-            panel = mbuf[i][place[t]]
-            if back:
-                panel = panel * live[t].astype(jnp.bfloat16)
-            arrived[t * width:(t + 1) * width, :] = panel
+        moved = []
+        for h in range(HALVES):
+            q = i * HALVES + h
+            for copy in sent[h]:
+                copy.wait_recv()
+            copies = []
+            for k, o in enumerate(offsets):
+                panel = gbuf[q][member_src[k]]
+                if o == 0:
+                    mbuf[q][k] = panel
+                else:
+                    msend[q][k] = panel
+                    step = members - o if back else o
+                    copies.append(send(msend[q].at[k], mbuf[q].at[k], ms_sem.at[q, k], mr_sem.at[q, k],
+                                       (g, lax.rem(m + step, members))))
+            moved.append(copies)
+        for h in range(HALVES):
+            q = i * HALVES + h
+            for copy in moved[h]:
+                copy.wait_recv()
+            for t in range(slots):
+                panel = mbuf[q][place[t]]
+                if back:
+                    panel = panel * live[t][:, lanes(h)].astype(jnp.bfloat16)
+                arrived[t * width:(t + 1) * width, lanes(h)] = panel
 
     def fold(x):
         y = jnp.sum(x.reshape(x.shape[0] // 8, 8, cols), axis=0)
@@ -103,16 +120,20 @@
     def all_sum(j, values):
         n = len(values)
         for q, value in enumerate(values):
-            sums[j][0, q * 8:(q + 1) * 8] = value
+            sums[j][0, q:q + 1] = jnp.sum(value, axis=0, keepdims=True)
 
         def put(r):
             return pltpu.make_async_remote_copy(
                 src_ref=sums[j].at[0], dst_ref=sums[j].at[r], send_sem=ss_sem.at[j],
                 recv_sem=sr_sem.at[j], device_id=peer(r), device_id_type=MESH)
 
-        @pl.loop(1, devices)
-        def _(r):
+        for r in range(1, min(devices, 64)):
             put(r).start()
+
+        if devices > 64:
+            @pl.loop(64, devices)
+            def _(r):
+                put(r).start()
 
         rest_of = sums[j].at[pl.ds(1, devices - 1)]
         whole = pltpu.make_async_remote_copy(
@@ -121,7 +142,7 @@
         whole.wait_recv()
         pending.append(whole)
         added = jnp.sum(sums[j][...], axis=0)
-        return [jnp.sum(added[q * 8:(q + 1) * 8]) for q in range(n)]
+        return [jnp.sum(added[q:q + 1]) for q in range(n)]
 
     def project(basis_t, value_ref):
         return jnp.dot(basis_t[...], value_ref[...], preferred_element_type=jnp.float32)
@@ -203,7 +224,7 @@
     slots = owners.shape[1]
     width = stack // slots
     devices = groups * members
-    offsets = tuple(range(members))
+    offsets = tuple(sorted(range(members), key=lambda o: -min(o, members - o)))
     dims = (groups, members, slots, width, rows, cols)
     f32, bf16 = jnp.float32, jnp.bfloat16
     vmem = pl.BlockSpec(memory_space=pltpu.VMEM)
@@ -217,10 +238,10 @@
         pltpu.VMEM((rows, cols), bf16), pltpu.VMEM((slots, width, cols), bf16),
         pltpu.VMEM((stack, cols), bf16), pltpu.VMEM((8, 128), f32),
     ]
-    scratch += [pltpu.VMEM((groups, width, cols), bf16)] * (2 * ROUTES)
-    scratch += [pltpu.VMEM((count, width, cols), bf16)] * (2 * ROUTES)
-    scratch += [pltpu.VMEM((devices, 8 * (1 + j % 2), 128), f32) for j in range(SUMS)]
-    scratch += [dma((ROUTES, groups)), dma((ROUTES, groups)), dma((ROUTES, count)), dma((ROUTES, count)),
+    scratch += [pltpu.VMEM((groups, width, cols // HALVES), bf16)] * (2 * PARTS)
+    scratch += [pltpu.VMEM((count, width, cols // HALVES), bf16)] * (2 * PARTS)
+    scratch += [pltpu.VMEM((devices, 1 + j % 2, 128), f32) for j in range(SUMS)]
+    scratch += [dma((PARTS, groups)), dma((PARTS, groups)), dma((PARTS, count)), dma((PARTS, count)),
                 dma((SUMS,)), dma((SUMS,))]
     lead = owners[0] // members
     shift = owners[0] % members

time: 133 us -> 124 us (0.932)
  Pallas kernels: 128 us -> 118 us
    pallas_call x1, Pallas kernels: 128 us -> 118 us  [on_device(): pl.pallas_call(functools.partial(kernel, dims, offsets), out_shape=(jax.S...]
    unnamed x4 -> x6, local copies, waits for them, and re-layouts: 3.12 us -> 3.68 us
where the time goes in v2:
time: 124 us
  Pallas kernels  118 us (95%)
  local copies, waits for them, and re-layouts  4.48 us (4%)
    pallas_call x1, Pallas kernels, on_device(): pl.pallas_call(functools.partial(kernel, dims, offsets), out_shape=(jax.S...  118 us
    unnamed x6, local copies, waits for them, and re-layouts  3.68 us

profile of v2, /device:TPU:0, one launch (start us, length us, event | category | flops | bytes accessed | tf_op | source)
XLA Modules:
  0.0 123.9 jit_solution(3458116369777837850)
XLA Ops:
  0.6 0.8 slice_reduce_fusion
  1.4 0.0 copy-start.1
  1.5 0.1 select_reduce_fusion
  1.5 0.6 copy-done.1
  2.1 0.2 fusion
  2.3 0.6 add_bitcast_fusion.tab_ref
  2.9 117.9 %shard_map.86 = (f32[1024,256]{1,0:T(8,128)}, bf16[1024,256]{1,0:T(8,128)(2,1)}) custom-call(s32[1,16]{1,0:T(1,128)} %add_bitcast_fusion.tab_ref, s32[1,4]{1,0:T(1,128)} %rank_ref.1, bf16[1024,512]{1,0:T(8,128)(2,1)} %v_ref.1, bf16[1024,512]{1,0:T(8,128)(2,1)} %u_ref.1, bf16[1024,256]{1,0:T(8,128)(2,1)} %x_ref.1, bf16[1024,256]{1,0:T(8,128)(2,1)} %obs_ref.1), custom_call_target="tpu_custom_call" | custom-call | flops 2684354560 | bytes 4194304 | tf_op jit(solution)/shard_map/pallas_call | solution.py:256
  120.8 0.0 copy-start
  120.8 2.3 %copy.11 = f32[1024,256]{1,0:T(8,128)} copy(f32[1024,256]{1,0:T(8,128)} %get-tuple-element.8) | data formatting | bytes 2097152
  123.1 0.0 copy-done
  123.1 0.8 copy.12
  (1 shorter events, 0.0 us)
Async XLA Ops:
  1.4 0.7 copy-start.1
  120.8 2.3 %copy-start = (bf16[1024,256]{1,0:T(8,128)(2,1)S(1)}, bf16[1024,256]{1,0:T(8,128)(2,1)}, u32[]{:S(2)}) copy-start(bf16[1024,256]{1,0:T(8,128)(2,1)} %get-tuple-element.9) | copy-start | bytes 1572868

commit v3 on v2

--- a/solution.py
+++ b/solution.py
@@ -117,7 +117,7 @@
         y = jnp.sum(x.reshape(x.shape[0] // 8, 8, cols), axis=0)
         return total(y[:, c:c + 128] for c in range(0, cols, 128))
 
-    def all_sum(j, values):
+    def all_sum(j, values, meanwhile=None):
         n = len(values)
         for q, value in enumerate(values):
             sums[j][0, q:q + 1] = jnp.sum(value, axis=0, keepdims=True)
@@ -135,6 +135,8 @@
             def _(r):
                 put(r).start()
 
+        if meanwhile is not None:
+            meanwhile()
         rest_of = sums[j].at[pl.ds(1, devices - 1)]
         whole = pltpu.make_async_remote_copy(
             src_ref=rest_of, dst_ref=rest_of, send_sem=ss_sem.at[j],
@@ -170,8 +172,9 @@
         part_sum = part_sum + fold(jnp.abs(r))
 
     entries = float(rows * cols * devices)
+    late = None
     for it in range(ITERS):
-        (spread,) = all_sum(2 * it, [part_sum])
+        (spread,) = all_sum(2 * it, [part_sum], late)
         scale = 1.345 * spread / entries + 1e-06
         for i in range(chunks):
             r = resid[at(i), :]
@@ -212,8 +215,13 @@
                 part_sum = part_sum + fold(jnp.abs(r))
             else:
                 out_ref[at(i), :] = r.astype(jnp.bfloat16)
-            before = x_ref[at(i), :].astype(jnp.float32) if it == 0 else model_ref[at(i), :]
-            model_ref[at(i), :] = before - step * grad[at(i), :]
+
+        def late(first=it == 0, step=step):
+            for i in range(chunks):
+                before = x_ref[at(i), :].astype(jnp.float32) if first else model_ref[at(i), :]
+                model_ref[at(i), :] = before - step * grad[at(i), :]
+
+    late()
     for copy in pending:
         copy.wait_send()
 

time: 124 us -> 124 us (level)
  no operation moved by 1% of the time
where the time goes in v3:
time: 124 us
  Pallas kernels  118 us (95%)
  local copies, waits for them, and re-layouts  4.48 us (4%)
    pallas_call x1, Pallas kernels, on_device(): pl.pallas_call(functools.partial(kernel, dims, offsets), out_shape=(jax.S...  118 us
    unnamed x6, local copies, waits for them, and re-layouts  3.68 us

profile of v3, /device:TPU:0, one launch (start us, length us, event | category | flops | bytes accessed | tf_op | source)
XLA Modules:
  0.0 123.7 jit_solution(385183767345781402)
XLA Ops:
  0.6 0.8 slice_reduce_fusion
  1.4 0.0 copy-start.1
  1.5 0.1 select_reduce_fusion
  1.5 0.6 copy-done.1
  2.1 0.2 fusion
  2.3 0.6 add_bitcast_fusion.tab_ref
  2.9 117.7 %shard_map.86 = (f32[1024,256]{1,0:T(8,128)}, bf16[1024,256]{1,0:T(8,128)(2,1)}) custom-call(s32[1,16]{1,0:T(1,128)} %add_bitcast_fusion.tab_ref, s32[1,4]{1,0:T(1,128)} %rank_ref.1, bf16[1024,512]{1,0:T(8,128)(2,1)} %v_ref.1, bf16[1024,512]{1,0:T(8,128)(2,1)} %u_ref.1, bf16[1024,256]{1,0:T(8,128)(2,1)} %x_ref.1, bf16[1024,256]{1,0:T(8,128)(2,1)} %obs_ref.1), custom_call_target="tpu_custom_call" | custom-call | flops 2684354560 | bytes 4194304 | tf_op jit(solution)/shard_map/pallas_call | solution.py:264
  120.6 0.0 copy-start
  120.6 2.3 %copy.11 = f32[1024,256]{1,0:T(8,128)} copy(f32[1024,256]{1,0:T(8,128)} %get-tuple-element.8) | data formatting | bytes 2097152
  123.0 0.0 copy-done
  123.0 0.8 copy.12
  (1 shorter events, 0.0 us)
Async XLA Ops:
  1.4 0.7 copy-start.1
  120.6 2.3 %copy-start = (bf16[1024,256]{1,0:T(8,128)(2,1)S(1)}, bf16[1024,256]{1,0:T(8,128)(2,1)}, u32[]{:S(2)}) copy-start(bf16[1024,256]{1,0:T(8,128)(2,1)} %get-tuple-element.9) | copy-start | bytes 1572868
